TPU v7x, 32 devices: a whole 2x2x4 slice. The times are simulated.
32 devices in a mesh: row: 8 (over z, x), col: 4 (over y, core).
Axes of the slice: x: 2, y: 2, z: 4, core: 2. Of those that a mesh axis runs over, the one named last changes fastest.
Arguments:
- density: float32 [10240, 10240], P('row', 'col'), may hold values from -6 to 6
- core_hamiltonian: float32 [10240, 10240], P('row', 'col'), may hold values from -6 to 6
- class_tables: float32 [4, 256, 256], replicated, may hold values from -0.375 to 0.375
- shell_scale: float32 [10240], replicated, may hold values from 0.5 to 1.5
- block_place: int32 [640], replicated, may hold values from 0 to 639, as said below
- work_blocks: int32 [32, 32], P(('row', 'col')), may hold values from 0 to 639, as said below
- quartet_bra: int32 [32, 512], P(('row', 'col')), may hold values from 0 to 1023
- quartet_ket: int32 [32, 512], P(('row', 'col')), may hold values from 0 to 1023
- quartet_class: int32 [32, 512], P(('row', 'col')), may hold values from 0 to 3
- quartet_factor: float32 [32, 512], P(('row', 'col')), may hold values from 0.25 to 1
- quartet_count: int32 [32], P(('row', 'col')), may hold values from 1 to 512, 5120 in all
Outputs:
- fock_matrix: float32 [10240, 10240], P('row', 'col')
Inputs may be any that keep to these rules, and one draw needn't show every extreme that they name: `block_place`: a permutation of the 640 shell blocks. `work_blocks`: each device's 32 shell blocks are distinct and listed in increasing block_place; exactly 4 of them have places in each run of 80 = 80 consecutive places from 0 (one block row of devices), and likewise exactly 8 in each run of 40 = 160 (one block column of devices).
All inputs are finite; a program needn't handle non-finite values. No bound on the sum of `quartet_count` on one device may be relied on, other than what follows from the above.
Results may differ from a plain program's by a relative error of at most 0.0003.
Values sent between devices are 32-bit elements; how exact they have to be, the bound alone decides.
A program may use at most 320 MiB of HBM per device.

v0:
```python
import jax
import jax.numpy as jnp
from jax import lax
from jax.sharding import PartitionSpec as P

SHELL = 16


ORDERS = (
    (3, 4, 0, 1, 2),
    (1, 2, 0, 3, 4),
    (2, 4, 0, 1, 3),
    (1, 3, 0, 2, 4),
    (2, 3, 0, 1, 4),
    (1, 4, 0, 2, 3),
)
COEFFS = (1.0, 1.0, -0.5, -0.5, -0.5, -0.5)


def make_class_stacks(class_tables):
    classes = class_tables.shape[0]
    pair_width = class_tables.shape[1]
    result = []
    for klass in range(classes):
        tensor = class_tables[klass].reshape(SHELL, SHELL, SHELL, SHELL)
        tables = []
        for layout in ORDERS:
            single = tuple((entry - 1 for entry in layout if entry != 0))
            tables.append(jnp.transpose(tensor, single).reshape(pair_width, pair_width))
        result.append(tables)
    return result


def pair_weights(weights):
    block_count = weights.shape[0]
    shell_width = weights.shape[1]
    outer = weights[:, None, :, None] * weights[None, :, None, :]
    return outer.reshape(block_count * block_count, shell_width * shell_width)


def class_terms(scaled, bra_pairs, ket_pairs, factors, tables, task_count):
    shell_a = bra_pairs // task_count
    shell_b = bra_pairs % task_count
    shell_c = ket_pairs // task_count
    shell_d = ket_pairs % task_count
    sources = (
        shell_c * task_count + shell_d,
        shell_a * task_count + shell_b,
        shell_b * task_count + shell_d,
        shell_a * task_count + shell_c,
        shell_b * task_count + shell_c,
        shell_a * task_count + shell_d,
    )
    targets = (sources[1], sources[0], sources[3], sources[2], sources[5], sources[4])
    values = []
    for source, table, weighting in zip(sources, tables, COEFFS):
        product = jnp.dot(scaled[source], table, precision=lax.Precision.HIGHEST)
        values.append(product * (weighting * factors)[:, None])
    return (jnp.concatenate(targets), jnp.concatenate(values))


def make_block_step(scaled, sorted_lists, tables, klass, block_rows, task_count):
    bra_pairs, ket_pairs, sorted_keys, factors = sorted_lists

    def block_step(block_index, running):
        offset = block_index * block_rows

        def window(values):
            return lax.dynamic_slice_in_dim(values, offset, block_rows, 0)

        keep = window(sorted_keys) == klass
        weighting = jnp.where(keep, window(factors), 0.0)
        targets, values = class_terms(
            scaled, window(bra_pairs), window(ket_pairs), weighting, tables, task_count
        )
        return running.at[targets].add(values)

    return block_step


def accumulate(totals, scaled, quartet_lists, begin_slot, end_slot, class_stacks, task_count):
    bra_pairs, ket_pairs, klasses, factors = quartet_lists
    slot_count = factors.shape[0]
    block_rows = min(slot_count, 128)
    classes = len(class_stacks)
    positions = jnp.arange(slot_count)
    inside = (positions >= begin_slot) & (positions < end_slot)
    sort_keys = jnp.where(inside, klasses, classes)
    order = jnp.argsort(sort_keys, stable=True)
    sorted_keys = sort_keys[order]
    sorted_lists = (
        bra_pairs[order],
        ket_pairs[order],
        sorted_keys,
        jnp.where(inside, factors, 0.0)[order],
    )
    class_counts = jnp.sum(
        (sorted_keys[None, :] == jnp.arange(classes)[:, None]).astype(jnp.int32), axis=1
    )
    class_ends = jnp.cumsum(class_counts)
    class_starts = class_ends - class_counts
    for klass in range(classes):
        step_fn = make_block_step(
            scaled, sorted_lists, class_stacks[klass], klass, block_rows, task_count
        )
        totals = lax.fori_loop(
            class_starts[klass] // block_rows,
            (class_ends[klass] + block_rows - 1) // block_rows,
            step_fn,
            totals,
        )
    return totals


def on_device(
    density,
    core_hamiltonian,
    class_tables,
    shell_scale,
    block_place,
    work_blocks,
    quartet_bra,
    quartet_ket,
    quartet_class,
    quartet_factor,
    quartet_count,
):
    row_count = lax.axis_size("row")
    col_count = lax.axis_size("col")
    task_count = work_blocks.shape[1]
    row_share = task_count // row_count
    col_share = task_count // col_count
    row_blocks = density.shape[0] // SHELL
    col_blocks = density.shape[1] // SHELL
    pair_width = SHELL * SHELL
    density_view = density.reshape(row_blocks, SHELL, col_blocks, SHELL)
    class_stacks = make_class_stacks(class_tables)
    scales = shell_scale.reshape(-1, SHELL)
    own_tasks = work_blocks[0]
    places = block_place[own_tasks]
    row_part = (places % row_blocks).reshape(row_count, row_share)
    col_part = (places % col_blocks).reshape(col_count, col_share)
    outgoing = jnp.concatenate(
        (
            jnp.broadcast_to(row_part[:, None, :], (row_count, col_count, row_share)),
            jnp.broadcast_to(col_part[None, :, :], (row_count, col_count, col_share)),
        ),
        axis=2,
    )
    incoming = lax.all_to_all(
        lax.all_to_all(outgoing, "row", split_axis=0, concat_axis=0, tiled=True),
        "col",
        split_axis=1,
        concat_axis=1,
        tiled=True,
    )
    wanted_rows = incoming[:, :, :row_share]
    wanted_cols = incoming[:, :, row_share:]
    row_index = jnp.transpose(wanted_rows, (0, 2, 1))[:, :, :, None]
    col_index = wanted_cols[:, None, :, :]
    layout = (row_count, row_share, col_count, col_share, pair_width)
    block_layout = (row_count, row_share, col_count, col_share, SHELL, SHELL)
    picked = density_view[row_index, :, col_index, :].reshape(layout)
    fetched = lax.all_to_all(
        lax.all_to_all(picked, "row", split_axis=0, concat_axis=0, tiled=True),
        "col",
        split_axis=2,
        concat_axis=2,
        tiled=True,
    )
    weights = pair_weights(scales[own_tasks])
    scaled = fetched.reshape(task_count * task_count, pair_width) * weights
    live_count = quartet_count[0]
    own_lists = (quartet_bra[0], quartet_ket[0], quartet_class[0], quartet_factor[0])
    zero_terms = jnp.zeros((task_count * task_count, pair_width), jnp.float32)
    fock_sums = jnp.zeros((row_blocks, SHELL, col_blocks, SHELL), jnp.float32)
    own_terms = accumulate(zero_terms, scaled, own_lists, 0, live_count, class_stacks, task_count)
    outbound = (own_terms * weights).reshape(layout)
    returned = lax.all_to_all(
        lax.all_to_all(outbound, "row", split_axis=0, concat_axis=0, tiled=True),
        "col",
        split_axis=2,
        concat_axis=2,
        tiled=True,
    )
    fock_sums = fock_sums.at[row_index, :, col_index, :].add(returned.reshape(block_layout))
    return core_hamiltonian + fock_sums.reshape(density.shape)


def solution(mesh):
    placed = (
        P("row", "col"),
        P("row", "col"),
        P(),
        P(),
        P(),
        P(("row", "col"), None),
        P(("row", "col"), None),
        P(("row", "col"), None),
        P(("row", "col"), None),
        P(("row", "col"), None),
        P(("row", "col")),
    )
    return jax.shard_map(
        on_device, mesh=mesh, in_specs=placed, out_specs=P("row", "col"), check_vma=False
    )
```

profile of v0, /device:TPU:0, one launch (start us, length us, event | category | flops | bytes accessed | tf_op | source)
XLA Modules:
  0.0 895.1 jit_solution(15577942352288241920)
XLA Ops:
  1.7 13.6 %all_to_all.30 = s32[8,4,12]{2,1,0:T(4,128)S(1)} all-to-all(s32[8,4,12]{2,1,0:T(4,128)S(1)} %pad_add_fusion.1), channel_id=1, replica_groups=mesh['row'=8,'col'=4] {'row'}, dimensions={0} | all-to-all | bytes 3072 | tf_op jit(solution)/shard_map/all_to_all | solution.py:151
  15.9 3.3 all-to-all-start.1
  19.1 58.5 %reshape.1349 = f32[80,16,160,16]{3,2,1,0:T(8,128)} reshape(f32[1280,2560]{1,0:T(8,128)} %param.19) | data formatting | bytes 26214400 | tf_op jit(solution)/shard_map/reshape | solution.py:136
  77.7 111.9 %copy.253 = f32[80,16,160,16]{3,1,2,0:T(8,128)} copy(f32[80,16,160,16]{3,2,1,0:T(8,128)} %reshape.1349) | data formatting | bytes 26214400 | tf_op jit(solution)/shard_map/reshape | solution.py:136
  191.2 20.0 %gather_fusion.28 = f32[1024,16,16]{2,1,0:T(8,128)} fusion(f32[80,16,160,16]{3,1,2,0:T(8,128)} %copy.253, s32[1024]{0:T(1024)S(1)} %reshape.1604), kind=kCustom, calls=%fused_computation.28 | custom fusion | bytes 2105344 | tf_op jit(solution)/shard_map/gather | solution.py:163
  211.2 7.0 reshape.1350
  218.1 3.7 all-to-all-start.2
  222.5 3.8 sort.17
  226.3 3.5 gather_fusion.25
  234.6 13.8 %all-to-all-done.2 = f32[8,4,4,8,256]{4,3,2,1,0:T(8,128)S(1)} async-done(((f32[8,4,4,8,256]{4,3,2,1,0:T(8,128)}), f32[8,4,4,8,256]{4,3,2,1,0:T(8,128)S(1)}, u32[]{:S(2)}, u32[]{:S(2)}) %all-to-all-start.2) | async-done | bytes 1048608 | tf_op jit(solution)/shard_map/all_to_all | solution.py:165
  249.5 4.5 all-to-all-start.3
  304.7 3.7 mul.478
  309.7 3.1 reshape.1354
  315.8 3.1 reshape.1356
  318.9 3.1 reshape.1357
  325.3 3.5 gather_fusion.30
  328.8 3.5 gather_fusion.26
  332.4 3.5 gather_fusion.27
  335.9 3.1 reshape.1359
  339.0 3.2 reshape.1360
  342.2 3.0 reshape.1361
  351.5 3.0 reshape.1364
  354.6 3.0 reshape.1365
  357.6 3.1 reshape.1366
  360.7 3.1 reshape.1367
  367.0 3.1 reshape.1369
  373.1 3.0 reshape.1371
  376.2 3.4 reshape.1372
  384.6 18.9 %while.52 = (s32[]{:T(128)}, f32[1024,256]{1,0:T(8,128)S(1)}, s32[]{:T(128)}, s32[512]{0:T(512)S(1)}, s32[512]{0:T(512)S(1)}, /*index=5*/f32[1024,256]{1,0:T(8,1...) while((s32[]{:T(128)}, f32[1024,256]{1,0:T(8,128)S(1)}, ...), condition=%wide.region_5.6_spmd, body=%wide.region_3.5_spmd.sunk | while | flops 604397568 | bytes 7142111 | solution.py:106
  397.0 6.5 scatter_fusion
  403.5 38.0 %while.53 = (s32[]{:T(128)}, f32[1024,256]{1,0:T(8,128)S(1)}, s32[]{:T(128)}, s32[512]{0:T(512)S(1)}, s32[512]{0:T(512)S(1)}, /*index=5*/f32[1024,256]{1,0:T(8,1...) while((s32[]{:T(128)}, f32[1024,256]{1,0:T(8,128)S(1)}, ...), condition=%wide.region_8.9_spmd, body=%wide.region_6.8_spmd.sunk | while | flops 604397568 | bytes 7142111 | solution.py:106
  415.9 6.5 scatter_fusion.1
  434.8 6.5 scatter_fusion.1
  441.4 37.8 %while.54 = (s32[]{:T(128)}, f32[1024,256]{1,0:T(8,128)S(1)}, s32[]{:T(128)}, s32[512]{0:T(512)S(1)}, s32[512]{0:T(512)S(1)}, /*index=5*/f32[1024,256]{1,0:T(8,1...) while((s32[]{:T(128)}, f32[1024,256]{1,0:T(8,128)S(1)}, ...), condition=%wide.region_11.12_spmd, body=%wide.region_9.11_spmd.sunk | while | flops 604397568 | bytes 7142111 | solution.py:106
  453.9 6.5 scatter_fusion.2
  472.7 6.5 scatter_fusion.2
  479.2 36.1 %while.55 = (s32[]{:T(128)}, f32[1024,256]{1,0:T(8,128)S(1)}, s32[]{:T(128)}, s32[512]{0:T(512)S(1)}, s32[512]{0:T(512)S(1)}, /*index=5*/f32[1024,256]{1,0:T(8,1...) while((s32[]{:T(128)}, f32[1024,256]{1,0:T(8,128)S(1)}, ...), condition=%wide.region_14.15_spmd, body=%wide.region_12.14_spmd.sunk | while | flops 604397568 | bytes 7142111 | solution.py:106
  490.7 6.5 scatter_fusion.3
  508.6 6.5 scatter_fusion.3
  517.5 28.4 %all_to_all.31 = f32[8,4,4,8,256]{4,3,2,1,0:T(8,128)S(1)} all-to-all(f32[8,4,4,8,256]{4,3,2,1,0:T(8,128)S(1)} %bitcast.399), channel_id=1, replica_groups=mesh['row'=8,'col'=4] {'row'}, dimensions={0} | all-to-all | bytes 2097152 | tf_op jit(solution)/shard_map/all_to_all | solution.py:180
  546.9 3.5 all-to-all-start.5
  551.0 13.9 %all-to-all-done.5 = f32[8,4,4,8,256]{4,3,1,0,2:T(8,128)S(1)} async-done(((f32[8,4,4,8,256]{4,3,1,0,2:T(8,128)}), f32[8,4,4,8,256]{4,3,1,0,2:T(8,128)S(1)}, u32[]{:S(2)}, u32[]{:S(2)}) %all-to-all-start.5) | async-done | bytes 1048608 | tf_op jit(solution)/shard_map/all_to_all | solution.py:179
  565.0 4.6 reshape.1660
  569.7 32.3 %broadcast.512 = f32[12800,16,16]{2,1,0:T(8,128)} broadcast(f32[]{:T(128)} %constant.545.clone.1), dimensions={} | broadcast | bytes 13107204
  602.0 124.2 %scatter_fusion.4 = f32[12800,16,16]{2,1,0:T(8,128)} fusion(f32[12800,16,16]{2,1,0:T(8,128)} %broadcast.512, s32[1024]{0:T(1024)S(1)} %reshape.1658, f32[1024,16,16]{2,1,0:T(8,128)} %reshape.1660), kind=kCustom, calls=%fused_computation.35 | custom fusion | flops 262144 | bytes 3149824
  726.1 70.1 %copy.284 = f32[80,16,160,16]{3,2,1,0:T(8,128)} copy(f32[80,16,160,16]{3,1,2,0:T(8,128)} %bitcast.70) | data formatting | bytes 26214400 | tf_op jit(solution)/shard_map/scatter-add | solution.py:186
  796.3 84.0 %reshape.1375 = f32[1280,2560]{1,0:T(8,128)} reshape(f32[80,16,160,16]{3,2,1,0:T(8,128)} %copy.284) | data formatting | bytes 26214400 | tf_op jit(solution)/shard_map/reshape | solution.py:187
  880.3 14.6 %add.658 = f32[1280,2560]{1,0:T(8,128)} add(f32[1280,2560]{1,0:T(8,128)} %param.20, f32[1280,2560]{1,0:T(8,128)} %reshape.1375) | non-fusion elementwise | flops 3276800 | bytes 39321600 | tf_op jit(solution)/shard_map/add | solution.py:187
  (300 shorter events, 161.1 us)
Async XLA Ops:
  0.0 0.7 copy-start
  15.9 173.7 %all-to-all-start.1 = ((s32[8,4,12]{2,0,1:T(8,128)}), s32[8,4,12]{2,0,1:T(8,128)S(1)}, u32[]{:S(2)}, u32[]{:S(2)}) async-start(s32[8,4,12]{2,0,1:T(8,128)} %copy.248), calls=%async_computation.1 | async-start | bytes 32768 | tf_op jit(solution)/shard_map/all_to_all | solution.py:150
  211.2 11.3 %copy-start.13 = (s32[1,512]{1,0:T(1,128)S(1)}, s32[1,512]{1,0:T(1,128)}, u32[]{:S(2)}) copy-start(s32[1,512]{1,0:T(1,128)} %param.27) | copy-start | bytes 6148
  218.1 35.9 %copy-start.9 = (f32[4,256,256]{2,1,0:T(8,128)S(1)}, f32[4,256,256]{2,1,0:T(8,128)}, u32[]{:S(2)}) copy-start(f32[4,256,256]{2,1,0:T(8,128)} %param.21) | copy-start | bytes 3145732
  218.1 30.3 %all-to-all-start.2 = ((f32[8,4,4,8,256]{4,3,2,1,0:T(8,128)}), f32[8,4,4,8,256]{4,3,2,1,0:T(8,128)S(1)}, u32[]{:S(2)}, u32[]{:S(2)}) async-start(f32[8,4,4,8,256]{4,3,2,1,0:T(8,128)} %reshape.1350), calls=%async_computation.2 | async-start | bytes 2097152 | tf_op jit(solution)/shard_map/all_to_all | solution.py:165
  249.5 133.4 %all-to-all-start.3 = ((f32[8,4,4,8,256]{4,3,1,0,2:T(8,128)}), f32[8,4,4,8,256]{4,3,1,0,2:T(8,128)}, u32[]{:S(2)}, u32[]{:S(2)}) async-start(f32[8,4,4,8,256]{4,3,1,0,2:T(8,128)} %copy.254), calls=%async_computation.3 | async-start | bytes 2097152 | tf_op jit(solution)/shard_map/all_to_all | solution.py:164
  255.7 6.6 copy-start.6
  268.0 6.6 copy-start.5
  280.0 6.6 copy-start.4
  296.7 4.5 copy-start.12
  308.4 7.4 copy-start.7
  315.8 9.5 %copy-start.14 = (f32[1,512]{1,0:T(1,128)S(1)}, f32[1,512]{1,0:T(1,128)}, u32[]{:S(2)}) copy-start(f32[1,512]{1,0:T(1,128)} %param.28) | copy-start | bytes 6148
  318.9 9.9 %copy-start.2 = (s32[1,512]{1,0:T(1,128)S(1)}, s32[1,512]{1,0:T(1,128)}, u32[]{:S(2)}) copy-start(s32[1,512]{1,0:T(1,128)} %param.25) | copy-start | bytes 6148
  318.9 13.4 %copy-start.3 = (s32[1,512]{1,0:T(1,128)S(1)}, s32[1,512]{1,0:T(1,128)}, u32[]{:S(2)}) copy-start(s32[1,512]{1,0:T(1,128)} %param.26) | copy-start | bytes 6148
  376.2 8.1 copy-start.8
  517.1 33.4 %copy-start.11 = (s32[8,4,4]{1,0,2:T(8,128)S(1)}, s32[8,4,4]{1,0,2:T(8,128)}, u32[]{:S(2)}) copy-start(s32[8,4,4]{1,0,2:T(8,128)} %get-tuple-element.1252) | copy-start | bytes 1540
  517.1 33.6 %copy-start.10 = (s32[8,4,8]{2,0,1:T(8,128)S(1)}, s32[8,4,8]{2,0,1:T(8,128)}, u32[]{:S(2)}) copy-start(s32[8,4,8]{2,0,1:T(8,128)} %get-tuple-element.1254) | copy-start | bytes 3076
  517.1 33.6 %copy-start.16 = (s32[2]{0:T(128)S(1)}, s32[2]{0:T(128)}, u32[]{:S(2)}) copy-start(s32[2]{0:T(128)} %constant.563) | copy-start | bytes 28
  517.1 33.7 %copy-start.15 = (s32[2]{0:T(128)S(1)}, s32[2]{0:T(128)}, u32[]{:S(2)}) copy-start(s32[2]{0:T(128)} %constant.566) | copy-start | bytes 28
  546.9 18.0 %all-to-all-start.5 = ((f32[8,4,4,8,256]{4,3,1,0,2:T(8,128)}), f32[8,4,4,8,256]{4,3,1,0,2:T(8,128)S(1)}, u32[]{:S(2)}, u32[]{:S(2)}) async-start(f32[8,4,4,8,256]{4,3,1,0,2:T(8,128)} %copy.281), calls=%async_computation.5 | async-start | bytes 2097152 | tf_op jit(solution)/shard_map/all_to_all | solution.py:179
  880.3 14.6 %copy-start.1 = (s32[640]{0:T(1024)S(1)}, s32[640]{0:T(1024)}, u32[]{:S(2)}) copy-start(s32[640]{0:T(1024)} %param.23) | copy-start | bytes 7684
where the time goes:
time: 910 us; the launch traced here: 895 us
  local copies, waits for them, and re-layouts  548 us (60%)
  other arithmetic  197 us (22%)
  matrix products  49.8 us (5%)
  blocking collectives  42 us (5%)
  waiting for transfers between devices  27.7 us (3%)
  starting transfers between devices  14.9 us (2%)
  between operations  13.8 us (2%)
    reshape x2, local copies, waits for them, and re-layouts, on_device(): density_view = density.reshape(row_blocks, SHELL, col_blocks, SHELL)  170 us
    unnamed x4, other arithmetic  124 us
    reshape x1, local copies, waits for them, and re-layouts, on_device(): return core_hamiltonian + fock_sums.reshape(density.shape)  84 us
    scatter-add x1, local copies, waits for them, and re-layouts, on_device(): fock_sums.at[row_index, :, col_index, :].add(returned.reshape(block_layout))  70.1 us
    reshape x24, local copies, waits for them, and re-layouts, make_class_stacks(): tables.append(jnp.transpose(tensor, single).reshape(pair_width, pair_width))  62.6 us
    dot_general x42, matrix products, class_terms(): product = jnp.dot(scaled[source], table, precision=lax.Precision.HIGHEST)  49.8 us
    scatter-add x7, other arithmetic, block_step(): return running.at[targets].add(values)  45.2 us
    another operation x20, local copies, waits for them, and re-layouts, make_class_stacks(): tensor = class_tables[klass].reshape(SHELL, SHELL, SHELL, SHELL)  36.9 us
  transfers between devices with their start and end apart: 4, of which 2 were waited for; matrix products, arithmetic and copies ran while one was open for 33% of the time, Pallas kernels for 0%

commit v1 on v0

v1 whole, which is shorter than its diff:
```python
import functools

import jax
import jax.numpy as jnp
from jax import lax
from jax.experimental import pallas as pl
from jax.experimental.pallas import tpu as pltpu
from jax.sharding import PartitionSpec as P

SHELL = 16
LANES = 128
GROUP = LANES // SHELL
CHUNK = 128
VMEM_LIMIT = 56 * 1024 * 1024
MESH = pl.DeviceIdType.MESH


def flat_index(cols):
    return lax.axis_index("row") * cols + lax.axis_index("col")


def coords(device, cols):
    return (device // cols, device % cols)


def slot_of(device, rows, cols):
    return (device % cols) * rows + device // cols


def greet_all(me, count, cols):
    barrier = pltpu.get_barrier_semaphore()

    def greet(step, carry):
        pl.semaphore_signal(
            barrier, inc=1, device_id=coords((me + step) % count, cols), device_id_type=MESH
        )
        return carry

    lax.fori_loop(1, count, greet, 0)
    pl.semaphore_wait(barrier, count - 1)


def share_kernel(rows, cols, work_ref, out_ref, send_sem, recv_sem):
    count = rows * cols
    me = flat_index(cols)
    greet_all(me, count, cols)

    def copy(step, slot):
        return pltpu.make_async_remote_copy(
            src_ref=work_ref,
            dst_ref=out_ref.at[slot],
            send_sem=send_sem.at[step],
            recv_sem=recv_sem.at[step],
            device_id=coords((me + step) % count, cols),
            device_id_type=MESH,
        )

    def send(step, carry):
        copy(step, me).start()
        return carry

    def finish(step, carry):
        copy(step, (me - step + count) % count).wait_recv()
        copy(step, me).wait_send()
        return carry

    lax.fori_loop(1, count, send, 0)
    out_ref[me] = work_ref[...]
    lax.fori_loop(1, count, finish, 0)


def exchange_kernel(rows, cols, src_ref, dst_ref, send_sem, recv_sem, own_sem):
    count = rows * cols
    me = flat_index(cols)
    greet_all(me, count, cols)

    def copy(step, slot):
        target = (me + step) % count
        return pltpu.make_async_remote_copy(
            src_ref=src_ref.at[slot_of(target, rows, cols)],
            dst_ref=dst_ref.at[slot],
            send_sem=send_sem.at[step],
            recv_sem=recv_sem.at[step],
            device_id=coords(target, cols),
            device_id_type=MESH,
        )

    own = slot_of(me, rows, cols)

    def send(step, carry):
        copy(step, own).start()
        return carry

    def finish(step, carry):
        copy(step, slot_of((me - step + count) % count, rows, cols)).wait_recv()
        copy(step, own).wait_send()
        return carry

    lax.fori_loop(1, count, send, 0)
    own_copy = pltpu.make_async_copy(src_ref.at[own], dst_ref.at[own], own_sem)
    own_copy.start()
    lax.fori_loop(1, count, finish, 0)
    own_copy.wait()


def lane_granule(rows):
    return lax.broadcasted_iota(jnp.int32, (rows, LANES), 1) // SHELL


def swap_granules(arrays):
    granule = lane_granule(arrays[0].shape[0])
    for distance in (4, 2, 1):
        keep = (granule & distance) == 0
        result = list(arrays)
        for i in range(GROUP):
            if i & distance == 0:
                low, high = arrays[i], arrays[i + distance]
                result[i] = jnp.where(keep, low, pltpu.roll(high, SHELL * distance, 1))
                result[i + distance] = jnp.where(
                    keep, pltpu.roll(low, LANES - SHELL * distance, 1), high
                )
        arrays = result
    return arrays


def places_of(device, place_ref, tasks_ref, row_share, col_share, row_blocks, col_blocks):
    row_base = lax.axis_index("row") * row_share
    col_base = lax.axis_index("col") * col_share
    row_starts, col_starts, col_offsets = [], [], []
    for r in range(row_share):
        place = place_ref[tasks_ref[device, 0, row_base + r]]
        row_starts.append(pl.multiple_of(lax.rem(place, row_blocks) * SHELL, SHELL))
    for k in range(col_share):
        place = lax.rem(place_ref[tasks_ref[device, 0, col_base + k]], col_blocks)
        col_starts.append(pl.multiple_of(lax.div(place, GROUP) * LANES, LANES))
        col_offsets.append(lax.rem(place, GROUP))
    return row_starts, col_starts, col_offsets


def copy_chunks(src_ref, dst_ref, sems):
    parts = sems.shape[0]
    height = dst_ref.shape[0] // parts
    copies = []
    for part in range(parts):
        window = pl.ds(part * height, height)
        pair = (src_ref.at[window], dst_ref.at[window])
        copies.append(pltpu.make_async_copy(pair[0], pair[1], sems.at[part]))
    for copy in copies:
        copy.start()
    for copy in copies:
        copy.wait()


def pack_kernel(
    rows, cols, row_share, col_share, place_ref, tasks_ref, density_ref, out_ref, held, sems
):
    copy_chunks(density_ref, held, sems)
    row_blocks, col_blocks = held.shape[0] // SHELL, held.shape[1] // SHELL
    granule = lane_granule(SHELL)

    def step(slot, carry):
        device = lax.rem(slot, rows) * cols + lax.div(slot, rows)
        row_starts, col_starts, col_offsets = places_of(
            device, place_ref, tasks_ref, row_share, col_share, row_blocks, col_blocks
        )
        slabs = [jnp.zeros((SHELL, LANES), jnp.float32)] * row_share
        for k in range(col_share):
            shift = lax.rem((k + GROUP - col_offsets[k]) * SHELL, LANES)
            for r in range(row_share):
                block = held[pl.ds(row_starts[r], SHELL), pl.ds(col_starts[k], LANES)]
                slabs[r] = jnp.where(granule == k, pltpu.roll(block, shift, 1), slabs[r])
        for r in range(row_share):
            out_ref[slot, pl.ds(r * SHELL, SHELL), :] = slabs[r]
        return carry

    lax.fori_loop(0, rows * cols, step, 0)


def place_kernel(
    rows, cols, row_share, col_share, place_ref, tasks_ref, parts_ref, core_ref, out_ref, held, sems
):
    copy_chunks(core_ref, held, sems)
    row_blocks, col_blocks = held.shape[0] // SHELL, held.shape[1] // SHELL
    granule = lane_granule(SHELL)

    def step(slot, carry):
        device = lax.rem(slot, rows) * cols + lax.div(slot, rows)
        row_starts, col_starts, col_offsets = places_of(
            device, place_ref, tasks_ref, row_share, col_share, row_blocks, col_blocks
        )
        slabs = [parts_ref[slot, pl.ds(r * SHELL, SHELL), :] for r in range(row_share)]
        for k in range(col_share):
            shift = lax.rem((col_offsets[k] + GROUP - k) * SHELL, LANES)
            windows = [
                (pl.ds(row_starts[r], SHELL), pl.ds(col_starts[k], LANES))
                for r in range(row_share)
            ]
            inside = granule == col_offsets[k]
            sums = [
                held[windows[r]] + jnp.where(inside, pltpu.roll(slabs[r], shift, 1), 0.0)
                for r in range(row_share)
            ]
            for r in range(row_share):
                held[windows[r]] = sums[r]
        return carry

    lax.fori_loop(0, rows * cols, step, 0)
    copy_chunks(held, out_ref, sems)


def split_bf16(values):
    high = values.astype(jnp.bfloat16)
    return high, (values - high.astype(jnp.float32)).astype(jnp.bfloat16)


def swap_table(half_ref, stage_ref):
    for a in range(SHELL // GROUP):
        for b in range(SHELL // GROUP):
            arrays = [
                half_ref[b, pl.ds(GROUP * a + i, SHELL, stride=SHELL), :] for i in range(GROUP)
            ]
            for j, array in enumerate(swap_granules(arrays)):
                stage_ref[a, pl.ds(GROUP * b + j, SHELL, stride=SHELL), :] = array


def table_stage(classes, tables_ref, half_ref, stage_ref, tab_ref):
    width = SHELL * SHELL
    row = lax.broadcasted_iota(jnp.int32, (width, width), 0)
    column = lax.broadcasted_iota(jnp.int32, (width, width), 1)
    swap = (row // SHELL == column % SHELL) & (row % SHELL == column // SHELL)
    swap = jnp.where(swap, 1.0, 0.0).astype(jnp.bfloat16)

    def keep(klass, form, values):
        high, low = split_bf16(values)
        tab_ref[klass, form, 0] = high
        tab_ref[klass, form, 1] = low
        return high, low

    def swapped(values):
        for half in range(2):
            half_ref[half] = values[:, half * LANES : (half + 1) * LANES]
        swap_table(half_ref, stage_ref)
        return -0.5 * jnp.concatenate([stage_ref[0], stage_ref[1]], axis=1)

    def step(klass, carry):
        values = tables_ref[klass]
        high, low = keep(klass, 0, values)
        keep(klass, 1, swapped(values))
        permuted = jnp.dot(high, swap, preferred_element_type=jnp.float32)
        permuted = permuted + jnp.dot(low, swap, preferred_element_type=jnp.float32)
        keep(klass, 2, swapped(permuted))
        return carry

    lax.fori_loop(0, classes, step, 0)


def quartet_kernel(
    classes, slots, task_count, col_share,
    work_ref, bra_ref, ket_ref, class_ref, factor_ref, count_ref,
    recv_ref, scale_ref, tables_ref, out_ref,
    half_ref, stage_ref, tab_ref, own_scale, left_ref, right_ref, x_ref, g_ref, y_ref, filled,
):
    width = SHELL * SHELL
    slabs = recv_ref.shape[0] // SHELL
    tiles = slabs // 8
    table_stage(classes, tables_ref, half_ref, stage_ref, tab_ref)

    def scale_step(u, carry):
        shell = work_ref[0, u]
        line = jnp.broadcast_to(scale_ref[pl.ds(lax.div(shell, GROUP), 1), :], (8, LANES))
        shift = lax.rem((GROUP - lax.rem(shell, GROUP)) * SHELL, LANES)
        own_scale[pl.ds(u, 1), :] = pltpu.roll(line, shift, 1)[0:1]
        return carry

    lax.fori_loop(0, task_count, scale_step, 0)
    source = lax.broadcasted_iota(jnp.int32, (LANES, LANES), 0)
    lane = lax.broadcasted_iota(jnp.int32, (LANES, LANES), 1)
    for half in range(2):
        spread = jnp.where(source == lane // SHELL + GROUP * half, 1.0, 0.0)
        left_ref[half] = jnp.dot(own_scale[...], spread, precision=lax.Precision.HIGHEST)
    repeat = jnp.where(source == lane % SHELL, 1.0, 0.0)
    right_ref[...] = jnp.dot(own_scale[...], repeat, precision=lax.Precision.HIGHEST)

    def tile_place(tile):
        u = pl.multiple_of(lax.rem(tile * 8, task_count), 8)
        return u, lax.div(tile * 8, task_count) * col_share

    def spread_step(tile, carry):
        u, v = tile_place(tile)
        for half in range(2):
            arrays = [
                recv_ref[pl.ds(tile * 8 * SHELL + GROUP * half + i, 8, stride=SHELL), :]
                for i in range(GROUP)
            ]
            arrays = swap_granules(arrays)
            left = left_ref[half, pl.ds(u, 8), :]
            for c in range(col_share):
                weight = left * right_ref[pl.ds(v + c, 1), :]
                x_ref[half, pl.ds(pl.multiple_of(c * slabs + tile * 8, 8), 8), :] = arrays[c] * weight
        return carry

    lax.fori_loop(0, tiles, spread_step, 0)

    def zero_step(tile, carry):
        for form in range(6):
            for half in range(2):
                y_ref[form, half, pl.ds(pl.multiple_of(tile * 8, 8), 8), :] = jnp.zeros(
                    (8, LANES), jnp.float32
                )
        return carry

    lax.fori_loop(0, tiles * col_share, zero_step, 0)
    for klass in range(classes):
        filled[klass] = 0

    def pairs_of(n):
        bra, ket = bra_ref[0, n], ket_ref[0, n]
        a, b = lax.div(bra, task_count), lax.rem(bra, task_count)
        c, d = lax.div(ket, task_count), lax.rem(ket, task_count)

        def at(v):
            return lax.rem(v, col_share) * slabs + lax.div(v, col_share) * task_count

        at_c, at_d = at(c), at(d)
        return c + at_d, a + at(b), b + at_d, a + at_c, b + at_c, a + at_d

    live = count_ref[0]

    def gather_step(n, carry):
        klass = class_ref[0, n]
        order = filled[klass]
        filled[klass] = order + 1
        row = klass * slots + order
        factor = factor_ref[0, n]
        sources = pairs_of(n)
        values = [
            [x_ref[half, pl.ds(sources[form], 1), :] * factor for half in range(2)]
            for form in range(6)
        ]
        for form in range(6):
            for half in range(2):
                g_ref[form, half, pl.ds(row, 1), :] = values[form][half]
        return carry

    lax.fori_loop(0, live, gather_step, 0)

    def class_step(klass, carry):
        def chunk_step(chunk, carry):
            rows = pl.ds(pl.multiple_of(klass * slots + chunk * CHUNK, CHUNK), CHUNK)
            for form in range(6):
                table_high = tab_ref[klass, form // 2, 0]
                table_low = tab_ref[klass, form // 2, 1]
                values = jnp.concatenate([g_ref[form, 0, rows, :], g_ref[form, 1, rows, :]], axis=1)
                high, low = split_bf16(values)
                dims = (((1,), (1 if form % 2 == 0 else 0,)), ((), ()))
                product = functools.partial(
                    lax.dot_general, dimension_numbers=dims, preferred_element_type=jnp.float32
                )
                result = product(high, table_high) + product(low, table_high)
                result = result + product(high, table_low)
                g_ref[form, 0, rows, :] = result[:, :LANES]
                g_ref[form, 1, rows, :] = result[:, LANES:]
            return carry

        return lax.fori_loop(0, lax.div(filled[klass] + CHUNK - 1, CHUNK), chunk_step, carry)

    lax.fori_loop(0, classes, class_step, 0)
    for klass in range(classes):
        filled[klass] = 0

    def scatter_step(n, carry):
        klass = class_ref[0, n]
        order = filled[klass]
        filled[klass] = order + 1
        row = klass * slots + order
        pairs = pairs_of(n)
        targets = (pairs[1], pairs[0], pairs[3], pairs[2], pairs[5], pairs[4])
        values = [
            [
                y_ref[form, half, pl.ds(targets[form], 1), :] + g_ref[form, half, pl.ds(row, 1), :]
                for half in range(2)
            ]
            for form in range(6)
        ]
        for form in range(6):
            for half in range(2):
                y_ref[form, half, pl.ds(targets[form], 1), :] = values[form][half]
        return carry

    lax.fori_loop(0, live, scatter_step, 0)

    def collect_step(tile, carry):
        u, v = tile_place(tile)
        for half in range(2):
            left = left_ref[half, pl.ds(u, 8), :]
            arrays = []
            for c in range(GROUP):
                if c < col_share:
                    window = pl.ds(pl.multiple_of(c * slabs + tile * 8, 8), 8)
                    total = y_ref[0, half, window, :]
                    for form in range(1, 6):
                        total = total + y_ref[form, half, window, :]
                    arrays.append(total * (left * right_ref[pl.ds(v + c, 1), :]))
                else:
                    arrays.append(jnp.zeros((8, LANES), jnp.float32))
            for i, array in enumerate(swap_granules(arrays)):
                out_ref[pl.ds(tile * 8 * SHELL + GROUP * half + i, 8, stride=SHELL), :] = array
        return carry

    lax.fori_loop(0, tiles, collect_step, 0)


def on_device(
    density,
    core_hamiltonian,
    class_tables,
    shell_scale,
    block_place,
    work_blocks,
    quartet_bra,
    quartet_ket,
    quartet_class,
    quartet_factor,
    quartet_count,
):
    rows = lax.axis_size("row")
    cols = lax.axis_size("col")
    count = rows * cols
    task_count = work_blocks.shape[1]
    row_share = task_count // rows
    col_share = task_count // cols
    classes = class_tables.shape[0]
    width = class_tables.shape[1]
    slots = quartet_bra.shape[1]
    message = (row_share * SHELL, LANES)
    messages = jax.ShapeDtypeStruct((count,) + message, jnp.float32)
    slab_rows = count * row_share * SHELL
    pair_rows = task_count * task_count

    vmem = pl.BlockSpec(memory_space=pltpu.VMEM)
    smem = pl.BlockSpec(memory_space=pltpu.SMEM)
    hbm = pl.BlockSpec(memory_space=pl.ANY)
    local = pltpu.CompilerParams(vmem_limit_bytes=VMEM_LIMIT)
    parts = 8

    def talk(collective_id):
        return pltpu.CompilerParams(collective_id=collective_id, has_side_effects=True)

    padded = jnp.pad(work_blocks, ((0, 0), (0, LANES - task_count)))
    tasks = pl.pallas_call(
        functools.partial(share_kernel, rows, cols),
        out_shape=jax.ShapeDtypeStruct((count, 1, LANES), jnp.int32),
        in_specs=[vmem],
        out_specs=vmem,
        scratch_shapes=[pltpu.SemaphoreType.DMA((count,)), pltpu.SemaphoreType.DMA((count,))],
        compiler_params=talk(0),
        name="share_tasks",
    )(padded)

    def exchange(collective_id, name, values):
        return pl.pallas_call(
            functools.partial(exchange_kernel, rows, cols),
            out_shape=messages,
            in_specs=[hbm],
            out_specs=hbm,
            scratch_shapes=[
                pltpu.SemaphoreType.DMA((count,)),
                pltpu.SemaphoreType.DMA((count,)),
                pltpu.SemaphoreType.DMA,
            ],
            compiler_params=talk(collective_id),
            name=name,
        )(values)

    sizes = (rows, cols, row_share, col_share)
    picked = pl.pallas_call(
        functools.partial(pack_kernel, *sizes),
        out_shape=messages,
        in_specs=[smem, smem, hbm],
        out_specs=vmem,
        scratch_shapes=[
            pltpu.VMEM(density.shape, jnp.float32),
            pltpu.SemaphoreType.DMA((parts,)),
        ],
        compiler_params=local,
        name="pack_density",
    )(block_place, tasks, density)
    fetched = exchange(1, "fetch_density", picked)

    terms = pl.pallas_call(
        functools.partial(quartet_kernel, classes, slots, task_count, col_share),
        out_shape=jax.ShapeDtypeStruct((slab_rows, LANES), jnp.float32),
        in_specs=[smem] * 6 + [vmem] * 3,
        out_specs=vmem,
        scratch_shapes=[
            pltpu.VMEM((2, width, LANES), jnp.float32),
            pltpu.VMEM((2, width, LANES), jnp.float32),
            pltpu.VMEM((classes, 3, 2, width, width), jnp.bfloat16),
            pltpu.VMEM((task_count, LANES), jnp.float32),
            pltpu.VMEM((2, task_count, LANES), jnp.float32),
            pltpu.VMEM((task_count, LANES), jnp.float32),
            pltpu.VMEM((2, pair_rows, LANES), jnp.float32),
            pltpu.VMEM((6, 2, classes * slots, LANES), jnp.float32),
            pltpu.VMEM((6, 2, pair_rows, LANES), jnp.float32),
            pltpu.SMEM((classes,), jnp.int32),
        ],
        compiler_params=local,
        name="quartets",
    )(
        work_blocks, quartet_bra, quartet_ket, quartet_class, quartet_factor, quartet_count,
        fetched.reshape(slab_rows, LANES),
        shell_scale.reshape(-1, LANES),
        class_tables,
    )
    returned = exchange(2, "return_fock", terms.reshape(messages.shape))

    return pl.pallas_call(
        functools.partial(place_kernel, *sizes),
        out_shape=jax.ShapeDtypeStruct(density.shape, jnp.float32),
        in_specs=[smem, smem, vmem, hbm],
        out_specs=hbm,
        scratch_shapes=[
            pltpu.VMEM(density.shape, jnp.float32),
            pltpu.SemaphoreType.DMA((parts,)),
        ],
        compiler_params=local,
        name="place_fock",
    )(block_place, tasks, returned, core_hamiltonian)


def solution(mesh):
    placed = (
        P("row", "col"),
        P("row", "col"),
        P(),
        P(),
        P(),
        P(("row", "col"), None),
        P(("row", "col"), None),
        P(("row", "col"), None),
        P(("row", "col"), None),
        P(("row", "col"), None),
        P(("row", "col")),
    )
    return jax.shard_map(
        on_device, mesh=mesh, in_specs=placed, out_specs=P("row", "col"), check_vma=False
    )
```

time: 910 us -> 153 us (0.17)
  the two profiles are of different devices: /device:TPU:0 before, /device:TPU:15 now
where the time goes in v1:
time: 153 us
  Pallas kernels  151 us (99%)
    pallas_call x2, Pallas kernels, exchange(): pl.pallas_call(functools.partial(exchange_kernel, rows, cols), out_shape=...  82.2 us
    pallas_call x1, Pallas kernels, on_device(): pl.pallas_call(functools.partial(quartet_kernel, classes, slots, task_cou...  30.3 us
    pallas_call x1, Pallas kernels, on_device(): pl.pallas_call(functools.partial(place_kernel, *sizes), out_shape=jax.Sha...  16.7 us
    pallas_call x1, Pallas kernels, on_device(): pl.pallas_call(functools.partial(pack_kernel, *sizes), out_shape=messages...  12.9 us
    pallas_call x1, Pallas kernels, on_device(): pl.pallas_call(functools.partial(share_kernel, rows, cols), out_shape=jax...  9.32 us

profile of v1, /device:TPU:15, one launch (start us, length us, event | category | flops | bytes accessed | tf_op | source)
XLA Modules:
  0.0 153.3 jit_solution(4210411878014331822)
XLA Ops:
  0.7 1.2 pad.4.work_ref
  1.8 9.3 %share_tasks.1.tasks_ref = s32[32,1,128]{2,1,0:T(1,128)} custom-call(s32[1,128]{1,0:T(1,128)} %pad.4.work_ref), custom_call_target="tpu_custom_call" | custom-call | tf_op jit(solution)/shard_map/share_tasks/pallas_call | solution.py:450
  11.1 12.9 %pack_density.1.src_ref = f32[32,64,128]{2,1,0:T(8,128)} custom-call(s32[640]{0:T(1024)} %place_ref.3, s32[32,1,128]{2,1,0:T(1,128)} %share_tasks.1.tasks_ref, f32[1280,2560]{1,0:T(8,128)} %density_ref.1), custom_call_target="tpu_custom_call" | custom-call | tf_op jit(solution)/shard_map/pack_density/pallas_call | solution.py:476
  24.1 30.4 %fetch_density.1 = f32[32,64,128]{2,1,0:T(8,128)} custom-call(f32[32,64,128]{2,1,0:T(8,128)} %pack_density.1.src_ref), custom_call_target="tpu_custom_call" | custom-call | tf_op jit(solution)/shard_map/fetch_density/pallas_call | solution.py:461
  54.5 30.3 %quartets.1 = f32[2048,128]{1,0:T(8,128)} custom-call(s32[1,32]{1,0:T(1,128)} %work_ref.1, s32[1,512]{1,0:T(1,128)} %bra_ref.1, s32[1,512]{1,0:T(1,128)} %ket_ref.1, s32[1,512]{1,0:T(1,128)} %class_ref.1, f32[1,512]{1,0:T(1,128)} %factor_ref.1, s32[1]{0:T(128)S(6)} %copy.12.count_ref, f32[2048,128]{1,0:T(8,128)} %bitcast.3, f32[80,128]{1,0:T(8,128)} %bitcast.5, ...), custom_call_target="tpu_custom_call" | custom-call | tf_op jit(solution)/shard_map/quartets/pallas_call | solution.py:490
  84.8 51.8 %return_fock.1.parts_ref = f32[32,64,128]{2,1,0:T(8,128)} custom-call(f32[32,64,128]{2,1,0:T(8,128)} %bitcast.4), custom_call_target="tpu_custom_call" | custom-call | tf_op jit(solution)/shard_map/return_fock/pallas_call | solution.py:461
  136.6 16.7 %place_fock.1 = f32[1280,2560]{1,0:T(8,128)} custom-call(s32[640]{0:T(1024)} %place_ref.3, s32[32,1,128]{2,1,0:T(1,128)} %share_tasks.1.tasks_ref, f32[32,64,128]{2,1,0:T(8,128)} %return_fock.1.parts_ref, f32[1280,2560]{1,0:T(8,128)} %core_ref.1), custom_call_target="tpu_custom_call" | custom-call | tf_op jit(solution)/shard_map/place_fock/pallas_call | solution.py:517

commit v2 on v1

v2 whole, which is shorter than its diff:
```python
import functools

import jax
import jax.numpy as jnp
from jax import lax
from jax.experimental import pallas as pl
from jax.experimental.pallas import tpu as pltpu
from jax.sharding import PartitionSpec as P

SHELL = 16
LANES = 128
GROUP = LANES // SHELL
CHUNK = 128
VMEM_LIMIT = 56 * 1024 * 1024
PACK_LIMIT = 24 * 1024 * 1024
QUARTET_LIMIT = 36 * 1024 * 1024
SMALL_LIMIT = 4 * 1024 * 1024
MESH = pl.DeviceIdType.MESH


def flat_index(cols):
    return lax.axis_index("row") * cols + lax.axis_index("col")


def coords(device, cols):
    return (device // cols, device % cols)


def slot_of(device, rows, cols):
    return (device % cols) * rows + device // cols


def greet_all(me, count, cols):
    barrier = pltpu.get_barrier_semaphore()

    def greet(step, carry):
        pl.semaphore_signal(
            barrier, inc=1, device_id=coords((me + step) % count, cols), device_id_type=MESH
        )
        return carry

    lax.fori_loop(1, count, greet, 0)
    pl.semaphore_wait(barrier, count - 1)


def share_kernel(rows, cols, task_count, work_ref, out_ref, line_ref, send_sem, recv_sem):
    count = rows * cols
    me = flat_index(cols)
    line_ref[...] = jnp.zeros_like(line_ref)
    line_ref[:, 0:task_count] = work_ref[...]
    greet_all(me, count, cols)

    def copy(step, slot):
        return pltpu.make_async_remote_copy(
            src_ref=line_ref,
            dst_ref=out_ref.at[slot],
            send_sem=send_sem.at[step],
            recv_sem=recv_sem.at[step],
            device_id=coords((me + step) % count, cols),
            device_id_type=MESH,
        )

    def send(step, carry):
        copy(step, me).start()
        return carry

    def finish(step, carry):
        copy(step, (me - step + count) % count).wait_recv()
        copy(step, me).wait_send()
        return carry

    lax.fori_loop(1, count, send, 0)
    out_ref[me] = line_ref[...]
    lax.fori_loop(1, count, finish, 0)


def exchange_kernel(rows, cols, src_ref, dst_ref, send_sem, recv_sem, own_sem, beside=None):
    count = rows * cols
    me = flat_index(cols)
    greet_all(me, count, cols)

    def copy(step, slot):
        target = (me + step) % count
        return pltpu.make_async_remote_copy(
            src_ref=src_ref.at[slot_of(target, rows, cols)],
            dst_ref=dst_ref.at[slot],
            send_sem=send_sem.at[step],
            recv_sem=recv_sem.at[step],
            device_id=coords(target, cols),
            device_id_type=MESH,
        )

    own = slot_of(me, rows, cols)

    def send(step, carry):
        copy(step, own).start()
        return carry

    def finish(step, carry):
        copy(step, slot_of((me - step + count) % count, rows, cols)).wait_recv()
        copy(step, own).wait_send()
        return carry

    lax.fori_loop(1, count, send, 0)
    own_copy = pltpu.make_async_copy(src_ref.at[own], dst_ref.at[own], own_sem)
    own_copy.start()
    if beside is not None:
        beside()
    lax.fori_loop(1, count, finish, 0)
    own_copy.wait()


def lane_granule(rows):
    return lax.broadcasted_iota(jnp.int32, (rows, LANES), 1) // SHELL


def swap_granules(arrays):
    granule = lane_granule(arrays[0].shape[0])
    for distance in (4, 2, 1):
        keep = (granule & distance) == 0
        result = list(arrays)
        for i in range(GROUP):
            if i & distance == 0:
                low, high = arrays[i], arrays[i + distance]
                result[i] = jnp.where(keep, low, pltpu.roll(high, SHELL * distance, 1))
                result[i + distance] = jnp.where(
                    keep, pltpu.roll(low, LANES - SHELL * distance, 1), high
                )
        arrays = result
    return arrays


def places_of(device, place_ref, tasks_ref, row_share, col_share, row_blocks, col_blocks):
    row, col = lax.axis_index("row"), lax.axis_index("col")
    row_starts, col_starts, col_offsets = [], [], []
    for r in range(row_share):
        place = place_ref[tasks_ref[device, 0, row * row_share + r]] - row * row_blocks
        row_starts.append(pl.multiple_of(place * SHELL, SHELL))
    for k in range(col_share):
        place = place_ref[tasks_ref[device, 0, col * col_share + k]] - col * col_blocks
        offset = place & (GROUP - 1)
        col_starts.append(pl.multiple_of((place - offset) * SHELL, LANES))
        col_offsets.append(offset)
    return row_starts, col_starts, col_offsets


def chunk_copies(src_ref, dst_ref, sems):
    parts = sems.shape[0]
    height = dst_ref.shape[0] // parts
    windows = [pl.ds(part * height, height) for part in range(parts)]
    return [
        pltpu.make_async_copy(src_ref.at[window], dst_ref.at[window], sems.at[part])
        for part, window in enumerate(windows)
    ]


def copy_chunks(src_ref, dst_ref, sems):
    copies = chunk_copies(src_ref, dst_ref, sems)
    for copy in copies:
        copy.start()
    for copy in copies:
        copy.wait()


def place_kernel(
    rows, cols, row_share, col_share, place_ref, tasks_ref, parts_ref, core_ref, out_ref, held, sems
):
    copy_chunks(core_ref, held, sems)
    row_blocks, col_blocks = held.shape[0] // SHELL, held.shape[1] // SHELL
    granule = lane_granule(SHELL)

    def step(slot, carry):
        device = lax.rem(slot, rows) * cols + lax.div(slot, rows)
        row_starts, col_starts, col_offsets = places_of(
            device, place_ref, tasks_ref, row_share, col_share, row_blocks, col_blocks
        )
        slabs = [parts_ref[slot, pl.ds(r * SHELL, SHELL), :] for r in range(row_share)]
        for k in range(col_share):
            shift = ((col_offsets[k] + GROUP - k) & (GROUP - 1)) * SHELL
            windows = [
                (pl.ds(row_starts[r], SHELL), pl.ds(col_starts[k], LANES))
                for r in range(row_share)
            ]
            inside = granule == col_offsets[k]
            sums = [
                held[windows[r]] + jnp.where(inside, pltpu.roll(slabs[r], shift, 1), 0.0)
                for r in range(row_share)
            ]
            for r in range(row_share):
                held[windows[r]] = sums[r]
        return carry

    lax.fori_loop(0, rows * cols, step, 0, unroll=2)
    copy_chunks(held, out_ref, sems)


def split_bf16(values):
    high = values.astype(jnp.bfloat16)
    return high, (values - high.astype(jnp.float32)).astype(jnp.bfloat16)


def swap_table(half_ref, stage_ref):
    for a in range(SHELL // GROUP):
        for b in range(SHELL // GROUP):
            arrays = [
                half_ref[b, pl.ds(GROUP * a + i, SHELL, stride=SHELL), :] for i in range(GROUP)
            ]
            for j, array in enumerate(swap_granules(arrays)):
                stage_ref[a, pl.ds(GROUP * b + j, SHELL, stride=SHELL), :] = array


def table_stage(classes, tables_ref, half_ref, stage_ref, tab_ref):
    width = SHELL * SHELL
    row = lax.broadcasted_iota(jnp.int32, (width, width), 0)
    column = lax.broadcasted_iota(jnp.int32, (width, width), 1)
    swap = (row // SHELL == column % SHELL) & (row % SHELL == column // SHELL)
    swap = jnp.where(swap, 1.0, 0.0).astype(jnp.bfloat16)

    def keep(klass, form, values):
        for turn, array in enumerate((values.T, values)):
            high, low = split_bf16(array)
            tab_ref[klass, form + turn, 0] = high
            tab_ref[klass, form + turn, 1] = low

    def swapped(values):
        for half in range(2):
            half_ref[half] = values[:, half * LANES : (half + 1) * LANES]
        swap_table(half_ref, stage_ref)
        return -0.5 * jnp.concatenate([stage_ref[0], stage_ref[1]], axis=1)

    def step(klass, carry):
        values = tables_ref[klass]
        keep(klass, 0, values)
        keep(klass, 2, swapped(values))
        high, low = split_bf16(values)
        permuted = jnp.dot(high, swap, preferred_element_type=jnp.float32)
        permuted = permuted + jnp.dot(low, swap, preferred_element_type=jnp.float32)
        keep(klass, 4, swapped(permuted))
        return carry

    lax.fori_loop(0, classes, step, 0)


def index_stage(classes, slots, task_count, col_share, slabs, bra, ket, klass, live, index_ref):
    a, b = bra // task_count, bra % task_count
    c, d = ket // task_count, ket % task_count

    def at(v):
        return (v % col_share) * slabs + (v // col_share) * task_count

    at_c, at_d = at(c), at(d)
    pairs = (c + at_d, a + at(b), b + at_d, a + at_c, b + at_c, a + at_d)
    for form in range(6):
        index_ref[form : form + 1, :] = 2 * pairs[form]
    lane = lax.broadcasted_iota(jnp.int32, (8, slots), 1)
    line = lax.broadcasted_iota(jnp.int32, (8, slots), 0)
    member = (jnp.broadcast_to(klass, (8, slots)) == line) & (lane < live)
    member = jnp.where(member, 1.0, 0.0)
    earlier = lax.broadcasted_iota(jnp.int32, (slots, slots), 0)
    later = lax.broadcasted_iota(jnp.int32, (slots, slots), 1)
    before = jnp.where(earlier < later, 1.0, 0.0).astype(jnp.bfloat16)
    ranks = jnp.dot(member.astype(jnp.bfloat16), before, preferred_element_type=jnp.float32)
    rank = jnp.sum(ranks * member, axis=0, keepdims=True).astype(jnp.int32)
    alive = lane[0:1] < live
    index_ref[6:7, :] = 2 * jnp.where(alive, klass * slots + rank, classes * slots)
    sizes = jnp.sum(member, axis=1, keepdims=True)
    sizes = jnp.sum(jnp.where(lane == line, sizes, 0.0), axis=0, keepdims=True)
    index_ref[7:8, :] = sizes.astype(jnp.int32)


def fetch_kernel(
    rows, cols, src_ref, tables_ref, dst_ref, tab_ref,
    half_ref, stage_ref, send_sem, recv_sem, own_sem,
):
    exchange_kernel(
        rows, cols, src_ref, dst_ref, send_sem, recv_sem, own_sem,
        lambda: table_stage(tables_ref.shape[0], tables_ref, half_ref, stage_ref, tab_ref),
    )


def pack_kernel(
    rows, cols, row_share, col_share, task_count, classes,
    place_ref, tasks_ref, count_ref, bra_ref, ket_ref, class_ref, held, out_ref, index_ref,
):
    index_stage(
        classes, bra_ref.shape[1], task_count, col_share, rows * cols * row_share,
        bra_ref[...], ket_ref[...], class_ref[...], count_ref[0], index_ref,
    )
    row_blocks, col_blocks = held.shape[0] // SHELL, held.shape[1] // SHELL
    granule = lane_granule(SHELL)

    def step(slot, carry):
        device = lax.rem(slot, rows) * cols + lax.div(slot, rows)
        row_starts, col_starts, col_offsets = places_of(
            device, place_ref, tasks_ref, row_share, col_share, row_blocks, col_blocks
        )
        slabs = [jnp.zeros((SHELL, LANES), jnp.float32)] * row_share
        for k in range(col_share):
            shift = ((k + GROUP - col_offsets[k]) & (GROUP - 1)) * SHELL
            for r in range(row_share):
                block = held[pl.ds(row_starts[r], SHELL), pl.ds(col_starts[k], LANES)]
                slabs[r] = jnp.where(granule == k, pltpu.roll(block, shift, 1), slabs[r])
        for r in range(row_share):
            out_ref[slot, pl.ds(r * SHELL, SHELL), :] = slabs[r]
        return carry

    lax.fori_loop(0, rows * cols, step, 0, unroll=2)


def quartet_kernel(
    classes, slots, task_count, col_share,
    work_ref, index_ref, factor_ref, count_ref, recv_ref, scale_ref, tab_ref, out_ref,
    own_scale, left_ref, right_ref, x_ref, g_ref, y_ref,
):
    slabs = recv_ref.shape[0] // SHELL
    tiles = slabs // 8

    def scale_step(u, carry):
        shell = work_ref[0, u]
        part = shell & (GROUP - 1)
        line = jnp.broadcast_to(scale_ref[pl.ds((shell - part) // GROUP, 1), :], (8, LANES))
        shift = ((GROUP - part) & (GROUP - 1)) * SHELL
        own_scale[pl.ds(u, 1), :] = pltpu.roll(line, shift, 1)[0:1]
        return carry

    lax.fori_loop(0, task_count, scale_step, 0, unroll=8)
    source = lax.broadcasted_iota(jnp.int32, (LANES, LANES), 0)
    lane = lax.broadcasted_iota(jnp.int32, (LANES, LANES), 1)
    for half in range(2):
        spread = jnp.where(source == lane // SHELL + GROUP * half, 1.0, 0.0)
        left_ref[half] = jnp.dot(own_scale[...], spread, precision=lax.Precision.HIGHEST)
    repeat = jnp.where(source == lane % SHELL, 1.0, 0.0)
    right_ref[...] = jnp.dot(own_scale[...], repeat, precision=lax.Precision.HIGHEST)

    def tile_place(tile):
        u = pl.multiple_of(lax.rem(tile * 8, task_count), 8)
        return u, lax.div(tile * 8, task_count) * col_share

    def pair_window(c, tile, half):
        return pl.ds(2 * (c * slabs + tile * 8) + half, 8, stride=2)

    def spread_step(tile, carry):
        u, v = tile_place(tile)
        for half in range(2):
            arrays = [
                recv_ref[pl.ds(tile * 8 * SHELL + GROUP * half + i, 8, stride=SHELL), :]
                for i in range(GROUP)
            ]
            arrays = swap_granules(arrays)
            left = left_ref[half, pl.ds(u, 8), :]
            for c in range(col_share):
                weight = left * right_ref[pl.ds(v + c, 1), :]
                x_ref[pair_window(c, tile, half), :] = arrays[c] * weight
        return carry

    lax.fori_loop(0, tiles, spread_step, 0, unroll=2)

    zero = jnp.zeros((64, LANES), jnp.float32)

    def zero_step(part, carry):
        for form in range(6):
            y_ref[form, pl.ds(pl.multiple_of(part * 64, 64), 64), :] = zero
        return carry

    lax.fori_loop(0, y_ref.shape[1] // 64, zero_step, 0)
    live = count_ref[0]
    batch = 4 if slots % 4 == 0 else 1
    batches = lax.div(live + batch - 1, batch)

    def pair(n, form):
        return pl.ds(pl.multiple_of(index_ref[form, n], 2), 2)

    def gather_step(step, carry):
        numbers = [step * batch + i for i in range(batch)]
        values = [[x_ref[pair(n, form), :] for form in range(6)] for n in numbers]
        for n, lines in zip(numbers, values):
            for form in range(6):
                g_ref[form, pair(n, 6), :] = lines[form]
        return carry

    lax.fori_loop(0, batches, gather_step, 0)

    def class_step(klass, carry):
        def chunk_step(chunk, carry):
            start = 2 * (klass * slots + chunk * CHUNK)
            windows = [pl.ds(start + half, CHUNK, stride=2) for half in range(2)]
            for form in range(6):
                values = jnp.concatenate([g_ref[form, window, :] for window in windows], axis=1)
                high, low = split_bf16(values)
                product = functools.partial(jnp.dot, preferred_element_type=jnp.float32)
                table_high = tab_ref[klass, form, 0]
                result = product(high, table_high) + product(low, table_high)
                result = result + product(high, tab_ref[klass, form, 1])
                for half in range(2):
                    g_ref[form, windows[half], :] = result[:, half * LANES : (half + 1) * LANES]
            return carry

        return lax.fori_loop(0, lax.div(index_ref[7, klass] + CHUNK - 1, CHUNK), chunk_step, carry)

    lax.fori_loop(0, classes, class_step, 0)

    def scatter_step(step, carry):
        numbers = [step * batch + i for i in range(batch)]
        terms = []
        for n in numbers:
            factor = jnp.where(n < live, factor_ref[0, n], 0.0)
            terms.append([g_ref[form, pair(n, 6), :] * factor for form in range(6)])
        for n, lines in zip(numbers, terms):
            targets = [pair(n, form ^ 1) for form in range(6)]
            sums = [y_ref[form, targets[form], :] + lines[form] for form in range(6)]
            for form in range(6):
                y_ref[form, targets[form], :] = sums[form]
        return carry

    lax.fori_loop(0, batches, scatter_step, 0)

    def collect_step(tile, carry):
        u, v = tile_place(tile)
        for half in range(2):
            left = left_ref[half, pl.ds(u, 8), :]
            arrays = []
            for c in range(GROUP):
                if c < col_share:
                    window = pair_window(c, tile, half)
                    total = y_ref[0, window, :]
                    for form in range(1, 6):
                        total = total + y_ref[form, window, :]
                    arrays.append(total * (left * right_ref[pl.ds(v + c, 1), :]))
                else:
                    arrays.append(jnp.zeros((8, LANES), jnp.float32))
            for i, array in enumerate(swap_granules(arrays)):
                out_ref[pl.ds(tile * 8 * SHELL + GROUP * half + i, 8, stride=SHELL), :] = array
        return carry

    lax.fori_loop(0, tiles, collect_step, 0, unroll=2)


def on_device(
    density,
    core_hamiltonian,
    class_tables,
    shell_scale,
    block_place,
    work_blocks,
    quartet_bra,
    quartet_ket,
    quartet_class,
    quartet_factor,
    quartet_count,
):
    rows = lax.axis_size("row")
    cols = lax.axis_size("col")
    count = rows * cols
    task_count = work_blocks.shape[1]
    row_share = task_count // rows
    col_share = task_count // cols
    classes = class_tables.shape[0]
    width = class_tables.shape[1]
    slots = quartet_bra.shape[1]
    message = (row_share * SHELL, LANES)
    messages = jax.ShapeDtypeStruct((count,) + message, jnp.float32)
    slab_rows = count * row_share * SHELL
    pair_rows = task_count * task_count

    vmem = pl.BlockSpec(memory_space=pltpu.VMEM)
    smem = pl.BlockSpec(memory_space=pltpu.SMEM)
    hbm = pl.BlockSpec(memory_space=pl.ANY)
    local = pltpu.CompilerParams(vmem_limit_bytes=VMEM_LIMIT)
    parts = 8

    def talk(collective_id, limit):
        return pltpu.CompilerParams(
            collective_id=collective_id, has_side_effects=True, vmem_limit_bytes=limit
        )

    def exchange(collective_id, name, values):
        return pl.pallas_call(
            functools.partial(exchange_kernel, rows, cols),
            out_shape=messages,
            in_specs=[hbm],
            out_specs=hbm,
            scratch_shapes=[
                pltpu.SemaphoreType.DMA((count,)),
                pltpu.SemaphoreType.DMA((count,)),
                pltpu.SemaphoreType.DMA,
            ],
            compiler_params=talk(collective_id, SMALL_LIMIT),
            name=name,
        )(values)

    sizes = (rows, cols, row_share, col_share)
    table_shape = (classes, 6, 2, width, width)
    tasks = pl.pallas_call(
        functools.partial(share_kernel, rows, cols, task_count),
        out_shape=jax.ShapeDtypeStruct((count, 1, LANES), jnp.int32),
        in_specs=[vmem],
        out_specs=vmem,
        scratch_shapes=[
            pltpu.VMEM((1, LANES), jnp.int32),
            pltpu.SemaphoreType.DMA((count,)),
            pltpu.SemaphoreType.DMA((count,)),
        ],
        compiler_params=talk(0, SMALL_LIMIT),
        name="share_tasks",
    )(work_blocks)
    picked, index = pl.pallas_call(
        functools.partial(pack_kernel, *sizes, task_count, classes),
        out_shape=(messages, jax.ShapeDtypeStruct((8, slots), jnp.int32)),
        in_specs=[smem] * 3 + [vmem] * 4,
        out_specs=(vmem, vmem),
        compiler_params=pltpu.CompilerParams(vmem_limit_bytes=PACK_LIMIT),
        name="pack_density",
    )(
        block_place, tasks, quartet_count, quartet_bra, quartet_ket, quartet_class, density
    )
    fetched, tables = pl.pallas_call(
        functools.partial(fetch_kernel, rows, cols),
        out_shape=(messages, jax.ShapeDtypeStruct(table_shape, jnp.bfloat16)),
        in_specs=[hbm, vmem],
        out_specs=(hbm, vmem),
        scratch_shapes=[
            pltpu.VMEM((2, width, LANES), jnp.float32),
            pltpu.VMEM((2, width, LANES), jnp.float32),
            pltpu.SemaphoreType.DMA((count,)),
            pltpu.SemaphoreType.DMA((count,)),
            pltpu.SemaphoreType.DMA,
        ],
        compiler_params=talk(1, PACK_LIMIT),
        name="fetch_density",
    )(picked, class_tables)

    terms = pl.pallas_call(
        functools.partial(quartet_kernel, classes, slots, task_count, col_share),
        out_shape=jax.ShapeDtypeStruct((slab_rows, LANES), jnp.float32),
        in_specs=[smem] * 4 + [vmem] * 3,
        out_specs=vmem,
        scratch_shapes=[
            pltpu.VMEM((task_count, LANES), jnp.float32),
            pltpu.VMEM((2, task_count, LANES), jnp.float32),
            pltpu.VMEM((task_count, LANES), jnp.float32),
            pltpu.VMEM((2 * pair_rows, LANES), jnp.float32),
            pltpu.VMEM((6, 2 * (classes * slots + CHUNK), LANES), jnp.float32),
            pltpu.VMEM((6, 2 * pair_rows, LANES), jnp.float32),
        ],
        compiler_params=pltpu.CompilerParams(vmem_limit_bytes=QUARTET_LIMIT),
        name="quartets",
    )(
        work_blocks, index, quartet_factor, quartet_count,
        fetched.reshape(slab_rows, LANES), shell_scale.reshape(-1, LANES), tables,
    )
    returned = exchange(2, "return_fock", terms.reshape(messages.shape))

    return pl.pallas_call(
        functools.partial(place_kernel, *sizes),
        out_shape=jax.ShapeDtypeStruct(density.shape, jnp.float32),
        in_specs=[smem, smem, vmem, hbm],
        out_specs=hbm,
        scratch_shapes=[
            pltpu.VMEM(density.shape, jnp.float32),
            pltpu.SemaphoreType.DMA((parts,)),
        ],
        compiler_params=local,
        name="place_fock",
    )(block_place, tasks, returned, core_hamiltonian)


def solution(mesh):
    placed = (
        P("row", "col"),
        P("row", "col"),
        P(),
        P(),
        P(),
        P(("row", "col"), None),
        P(("row", "col"), None),
        P(("row", "col"), None),
        P(("row", "col"), None),
        P(("row", "col"), None),
        P(("row", "col")),
    )
    return jax.shard_map(
        on_device, mesh=mesh, in_specs=placed, out_specs=P("row", "col"), check_vma=False
    )
```

time: 153 us -> 117 us (0.76)
  Pallas kernels: 151 us -> 106 us
  local copies, waits for them, and re-layouts: 1.17 us -> 9.08 us
    pallas_call x2 -> x1, Pallas kernels: 82.2 us -> 33.9 us  [exchange(): pl.pallas_call(functools.partial(exchange_kernel, rows, cols), out_shape=...]
    pallas_call x2 -> x3, Pallas kernels: 22.3 us -> 43 us  [the longest x1 30 us: on_device(): pl.pallas_call(functools.partial(fetch_kernel, rows, cols), out_shape=(me...]
    pallas_call x1, Pallas kernels: 30.3 us -> 14.5 us  [on_device(): pl.pallas_call(functools.partial(quartet_kernel, classes, slots, task_cou...]
    unnamed x0 -> x24, local copies, waits for them, and re-layouts: none -> 9.08 us
    pallas_call x1, Pallas kernels: 16.7 us -> 14.8 us  [on_device(): pl.pallas_call(functools.partial(place_kernel, *sizes), out_shape=jax.Sha...]
where the time goes in v2:
time: 117 us; the launch traced here: 116 us
  Pallas kernels  106 us (91%)
  local copies, waits for them, and re-layouts  9.08 us (8%)
    pallas_call x1, Pallas kernels, exchange(): pl.pallas_call(functools.partial(exchange_kernel, rows, cols), out_shape=...  33.9 us
    pallas_call x1, Pallas kernels, on_device(): pl.pallas_call(functools.partial(fetch_kernel, rows, cols), out_shape=(me...  30 us
    pallas_call x1, Pallas kernels, on_device(): pl.pallas_call(functools.partial(place_kernel, *sizes), out_shape=jax.Sha...  14.8 us
    pallas_call x1, Pallas kernels, on_device(): pl.pallas_call(functools.partial(quartet_kernel, classes, slots, task_cou...  14.5 us
    unnamed x24, local copies, waits for them, and re-layouts  9.08 us
    pallas_call x1, Pallas kernels, on_device(): pl.pallas_call(functools.partial(share_kernel, rows, cols, task_count), o...  8.06 us
    pallas_call x1, Pallas kernels, on_device(): pl.pallas_call(functools.partial(pack_kernel, *sizes, task_count, classes...  4.94 us

profile of v2, /device:TPU:15, one launch (start us, length us, event | category | flops | bytes accessed | tf_op | source)
XLA Modules:
  0.0 116.1 jit_solution(10204317063377444262)
XLA Ops:
  0.0 0.0 copy-start.10
  0.0 0.0 copy-start.11
  0.7 0.0 copy-start.9
  0.7 0.6 copy-done.9
  1.3 8.1 %share_tasks.1.tasks_ref = s32[32,1,128]{2,1,0:T(1,128)S(1)} custom-call(s32[1,32]{1,0:T(1,128)S(1)} %copy-done.9), custom_call_target="tpu_custom_call" | custom-call | tf_op jit(solution)/shard_map/share_tasks/pallas_call | solution.py:493
  9.4 0.0 copy-start
  9.4 4.7 %copy-done = f32[1280,2560]{1,0:T(8,128)S(1)} copy-done((f32[1280,2560]{1,0:T(8,128)S(1)}, f32[1280,2560]{1,0:T(8,128)}, u32[]{:S(2)}) %copy-start) | copy-done | bytes 13107224
  14.1 0.0 copy-start.5
  14.1 0.7 copy-done.5
  14.8 0.0 copy-start.6
  14.8 0.7 copy-done.6
  15.5 0.0 copy-start.7
  15.5 0.7 copy-done.7
  16.2 0.0 copy-start.8
  16.2 0.7 copy-done.8
  16.9 0.0 copy-start.3
  16.9 0.0 copy-start.2
  16.9 0.0 copy-start.4
  16.9 4.9 %pack_density.1 = (f32[32,64,128]{2,1,0:T(8,128)S(1)}, s32[8,512]{1,0:T(8,128)S(1)}) custom-call(s32[640]{0:T(1024)S(1)} %copy-done.5, s32[32,1,128]{2,1,0:T(1,128)S(1)} %share_tasks.1.tasks_ref, s32[1]{0:T(128)S(6)} %copy.12.count_ref, s32[1,512]{1,0:T(1,128)S(1)} %copy-done.6, s32[1,512]{1,0:T(1,128)S(1)} %copy-done.7, s32[1,512]{1,0:T(1,128)S(1)} %copy-done.8, ...), custom_call_target="tpu_custom_call" | custom-call | tf_op jit(solution)/shard_map/pack_density/pallas_call | solution.py:506
  21.8 0.0 copy-done.2
  21.8 30.0 %fetch_density.1 = (f32[32,64,128]{2,1,0:T(8,128)S(1)}, bf16[4,6,2,256,256]{4,3,2,1,0:T(8,128)(2,1)S(1)}) custom-call(f32[32,64,128]{2,1,0:T(8,128)S(1)} %get-tuple-element.10.src_ref, f32[4,256,256]{2,1,0:T(8,128)S(1)} %copy-done.2), custom_call_target="tpu_custom_call" | custom-call | tf_op jit(solution)/shard_map/fetch_density/pallas_call | solution.py:516
  51.9 0.0 copy-done.10
  51.9 0.0 copy-done.11
  51.9 0.0 copy-done.4
  51.9 14.5 %quartets.1 = f32[2048,128]{1,0:T(8,128)S(1)} custom-call(s32[1,32]{1,0:T(1,128)S(1)} %copy-done.10, s32[8,512]{1,0:T(8,128)S(1)} %get-tuple-element.9.index_ref, f32[1,512]{1,0:T(1,128)S(1)} %copy-done.11, s32[1]{0:T(128)S(6)} %copy.12.count_ref, f32[2048,128]{1,0:T(8,128)S(1)} %bitcast.4, f32[80,128]{1,0:T(8,128)S(1)} %bitcast.5, ...), custom_call_target="tpu_custom_call" | custom-call | tf_op jit(solution)/shard_map/quartets/pallas_call | solution.py:532
  66.4 33.9 %return_fock.1.parts_ref = f32[32,64,128]{2,1,0:T(8,128)S(1)} custom-call(f32[32,64,128]{2,1,0:T(8,128)S(1)} %bitcast.3), custom_call_target="tpu_custom_call" | custom-call | tf_op jit(solution)/shard_map/return_fock/pallas_call | solution.py:477
  100.3 0.0 copy-done.3
  100.3 0.0 copy-start.1
  100.3 1.0 copy-done.1
  101.3 14.8 %place_fock.1 = f32[1280,2560]{1,0:T(8,128)} custom-call(s32[640]{0:T(1024)} %place_ref.3, s32[32,1,128]{2,1,0:T(1,128)} %copy-done.3, f32[32,64,128]{2,1,0:T(8,128)} %copy-done.1, f32[1280,2560]{1,0:T(8,128)} %core_ref.1), custom_call_target="tpu_custom_call" | custom-call | tf_op jit(solution)/shard_map/place_fock/pallas_call | solution.py:553
Async XLA Ops:
  0.0 51.9 %copy-start.10 = (s32[1,32]{1,0:T(1,128)S(1)}, s32[1,32]{1,0:T(1,128)}, u32[]{:S(2)}) copy-start(s32[1,32]{1,0:T(1,128)} %work_ref.3) | copy-start | bytes 388
  0.0 51.9 %copy-start.11 = (f32[1,512]{1,0:T(1,128)S(1)}, f32[1,512]{1,0:T(1,128)}, u32[]{:S(2)}) copy-start(f32[1,512]{1,0:T(1,128)} %factor_ref.1) | copy-start | bytes 6148
  0.7 0.7 copy-start.9
  9.4 4.7 %copy-start = (f32[1280,2560]{1,0:T(8,128)S(1)}, f32[1280,2560]{1,0:T(8,128)}, u32[]{:S(2)}) copy-start(f32[1280,2560]{1,0:T(8,128)} %held.1) | copy-start | bytes 39321604
  14.1 0.7 copy-start.5
  14.8 0.7 copy-start.6
  15.5 0.7 copy-start.7
  16.2 0.7 copy-start.8
  16.9 83.4 %copy-start.3 = (s32[32,1,128]{2,1,0:T(1,128)}, s32[32,1,128]{2,1,0:T(1,128)S(1)}, u32[]{:S(2)}) copy-start(s32[32,1,128]{2,1,0:T(1,128)S(1)} %share_tasks.1.tasks_ref) | copy-start | bytes 49156
  16.9 5.0 %copy-start.2 = (f32[4,256,256]{2,1,0:T(8,128)S(1)}, f32[4,256,256]{2,1,0:T(8,128)}, u32[]{:S(2)}) copy-start(f32[4,256,256]{2,1,0:T(8,128)} %tables_ref.1) | copy-start | bytes 3145732
  16.9 35.0 %copy-start.4 = (f32[10240]{0:T(1024)S(1)}, f32[10240]{0:T(1024)}, u32[]{:S(2)}) copy-start(f32[10240]{0:T(1024)} %param.14) | copy-start | bytes 122884
  100.3 1.0 copy-start.1
